TPU v7x, 32 devices: a whole 2x2x4 slice. The times are simulated.
32 devices in a mesh: row: 4 (over y, x), col: 8 (over z, core).
Axes of the slice: x: 2, y: 2, z: 4, core: 2. Of those that a mesh axis runs over, the one named last changes fastest.
Arguments:
- features: bfloat16 [32768, 128], P(('col', 'row')), may hold values from -6 to 6
- tiles: bfloat16 [4, 8, 512, 128, 128], P('row', 'col'), may hold values from -0.21875 to 0.21875
- tile_rows: int32 [4, 8, 512], P('row', 'col'), may hold values from 0 to 63
- tile_cols: int32 [4, 8, 512], P('row', 'col'), may hold values from 0 to 31
- tile_counts: int32 [4, 8], P('row', 'col'), may hold values from 128 to 512, as said below
- weight: bfloat16 [128, 128], replicated, may hold values from -0.5 to 0.5
- bias: float32 [128], replicated, may hold values from -3 to 3
Outputs:
- hidden: bfloat16 [32768, 128], P(('row', 'col'))
Inputs may be any that keep to these rules, and one draw needn't show every extreme that they name: `tile_counts`: some grid cell has exactly 512 live slots in every draw.
All inputs are finite; a program needn't handle non-finite values.
Results may differ from a plain program's by a relative error of at most 0.014.
Values may be sent and summed in bfloat16 or wider, within the bound.
A program may use at most 192 MiB of HBM per device.

v0:
```python
import jax
import jax.numpy as jnp
from jax import lax
from jax.sharding import PartitionSpec as P


def local(features, tiles, tile_rows, tile_cols, tile_counts, weight, bias):
    slots_n = tiles.shape[2]
    width = features.shape[1]
    cell = tiles.reshape(slots_n, 128, 128)
    rows = tile_rows.reshape(slots_n)
    cols = tile_cols.reshape(slots_n)
    band = lax.all_gather(features, "row", axis=0, tiled=True)
    col_blocks = band.shape[0] // 128
    band_flat = band.reshape(col_blocks, 128 * width)
    col_select = (cols[:, None] == jnp.arange(col_blocks, dtype=jnp.int32)[None, :]).astype(
        jnp.bfloat16
    )
    picked = jnp.dot(col_select, band_flat, preferred_element_type=jnp.float32).astype(jnp.bfloat16)
    picked = picked.reshape(slots_n, 128, width)
    prod = jnp.einsum("tij,tjf->tif", cell, picked, preferred_element_type=jnp.float32)
    own_rows = features.shape[0]
    band_rows = own_rows * lax.axis_size("col")
    row_blocks = band_rows // 128
    live = jnp.arange(slots_n, dtype=jnp.int32) < tile_counts[0, 0]
    row_select = (
        (jnp.arange(row_blocks, dtype=jnp.int32)[:, None] == rows[None, :]) & live[None, :]
    ).astype(jnp.float32)
    partial_value = jnp.dot(
        row_select,
        prod.reshape(slots_n, 128 * width),
        precision=lax.Precision.HIGHEST,
        preferred_element_type=jnp.float32,
    )
    partial_value = partial_value.reshape(band_rows, width)
    summed = lax.psum_scatter(
        partial_value.astype(jnp.bfloat16), "col", scatter_dimension=0, tiled=True
    )
    mixed = jnp.dot(summed, weight, preferred_element_type=jnp.float32) + bias
    return jnp.maximum(mixed, 0.0).astype(jnp.bfloat16)


def solution(mesh):
    in_specs = (
        P(("col", "row"), None),
        P("row", "col", None, None, None),
        P("row", "col", None),
        P("row", "col", None),
        P("row", "col"),
        P(),
        P(),
    )
    out_specs = P(("row", "col"), None)
    return jax.shard_map(local, mesh=mesh, in_specs=in_specs, out_specs=out_specs, check_vma=False)
```

profile of v0, /device:TPU:0, one launch (start us, length us, event | category | flops | bytes accessed | tf_op | source)
XLA Modules:
  0.0 182.4 jit_solution(15912838485891707466)
XLA Ops:
  6.5 0.0 copy-start
  6.5 0.0 all-gather.2.cloned.1.call-start
  6.5 0.7 all-gather.2.cloned.1.call-update
  7.3 0.0 reduce-scatter.2.cloned.1.call-start
  8.0 30.6 %all-gather.2.cloned.1.call-done = bf16[4096,128]{1,0:T(8,128)(2,1)} async-done(((bf16[1024,128]{1,0:T(8,128)(2,1)}), bf16[4096,128]{1,0:T(8,128)(2,1)}) %all-gather.2.cloned.1.call-update) | async-done | bytes 1048592 | tf_op jit(solution)/shard_map/all_gather | solution.py:13
  38.6 1.5 reshape.21
  40.1 5.5 %fusion.5 = bf16[64,8,128,128]{3,1,2,0:T(8,128)(2,1)S(1)} fusion(bf16[32,16384]{1,0:T(8,128)(2,1)S(1)} %reshape.21, s32[512]{0:T(512)} %bitcast.22), kind=kOutput, calls=%fused_computation.5 | convolution fusion | flops 545275904 | bytes 17827840 | tf_op jit(solution)/shard_map/dot_general | solution.py:19
  45.6 8.3 %copy.12 = bf16[64,8,128,128]{3,2,1,0:T(8,128)(2,1)} copy(bf16[64,8,128,128]{3,1,2,0:T(8,128)(2,1)S(1)} %fusion.5) | data formatting | bytes 33554432
  53.9 25.2 %fusion.2 = f32[512,128,128]{1,2,0:T(8,128)} fusion(bf16[512,128,128]{2,1,0:T(8,128)(2,1)} %bitcast.21, bf16[1,1,512,128,128]{4,3,2,1,0:T(8,128)(2,1)} %param.8), kind=kOutput, calls=%fused_computation.4 | convolution fusion | flops 2147483648 | bytes 67108864 | tf_op jit(solution)/shard_map/tij,tjf->tif/dot_general | solution.py:21
  79.1 0.0 copy-start.1
  79.1 34.8 %copy.10 = f32[512,128,128]{0,2,1:T(8,128)} copy(f32[512,128,128]{1,2,0:T(8,128)} %fusion.2) | data formatting | bytes 67108864 | tf_op jit(solution)/shard_map/tij,tjf->tif/dot_general | solution.py:21
  113.9 0.0 copy-done.1
  113.9 0.0 copy-start.2
  113.9 21.5 %convolution_convert_fusion.1 = bf16[64,16384]{1,0:T(8,128)(2,1)S(1)} fusion(f32[512,16384]{0,1:T(8,128)} %bitcast.20, s32[512]{0:T(512)S(1)} %bitcast.23, pred[512]{0:T(512)(128)(4,1)S(1)} %iota_compare_fusion.3), kind=kOutput, calls=%fused_computation.1 | convolution fusion | flops 6443565056 | bytes 35654144 | tf_op jit(solution)/shard_map/dot_general | solution.py:29
  135.4 2.4 %convert_element_type.16 = bf16[8192,128]{1,0:T(8,128)(2,1)} reshape(bf16[64,16384]{1,0:T(8,128)(2,1)S(1)} %convolution_convert_fusion.1) | data formatting | bytes 4194304 | tf_op jit(solution)/shard_map/convert_element_type | solution.py:37
  137.7 0.0 reduce-scatter.2.cloned.1.call-update
  137.8 35.9 %reduce-scatter.2.cloned.1.call-done = bf16[1024,128]{1,0:T(8,128)(2,1)} async-done(((bf16[8192,128]{1,0:T(8,128)(2,1)}), bf16[1024,128]{1,0:T(8,128)(2,1)}) %reduce-scatter.2.cloned.1.call-update) | async-done | bytes 262160 | tf_op jit(solution)/shard_map/reduce_scatter | solution.py:36
  173.7 0.0 copy-done
  173.7 0.0 copy-done.2
  173.7 1.9 %fusion.7 = bf16[1024,128]{1,0:T(8,128)(2,1)} fusion(bf16[1024,128]{1,0:T(8,128)(2,1)} %reduce-scatter.2.cloned.1.call-done, bf16[128,128]{1,0:T(8,128)(2,1)S(1)} %copy-done, f32[128]{0:T(128)S(1)} %copy-done.2), kind=kOutput, calls=%fused_computation.8 | convolution fusion | flops 33947648 | bytes 557568 | tf_op jit(solution)/shard_map/dot_general | solution.py:39
  (1 shorter events, 0.0 us)
Async XLA Ops:
  6.5 167.1 %copy-start = (bf16[128,128]{1,0:T(8,128)(2,1)S(1)}, bf16[128,128]{1,0:T(8,128)(2,1)}, u32[]{:S(2)}) copy-start(bf16[128,128]{1,0:T(8,128)(2,1)} %param.12) | copy-start | bytes 98308
  6.5 32.0 %all-gather.2.cloned.1.call-start = ((), (), s32[]{:S(2)}) async-start(), calls=%async_computation.1 | async-start | bytes 1310720 | tf_op jit(solution)/shard_map/all_gather | solution.py:13
  7.3 166.4 %reduce-scatter.2.cloned.1.call-start = ((), (), s32[]{:S(2)}) async-start(), calls=%async_computation.2 | async-start | bytes 2359296 | tf_op jit(solution)/shard_map/reduce_scatter | solution.py:36
  79.1 34.8 %copy-start.1 = (s32[1,1,512]{2,1,0:T(1,128)S(1)}, s32[1,1,512]{2,1,0:T(1,128)}, u32[]{:S(2)}) copy-start(s32[1,1,512]{2,1,0:T(1,128)} %param.9) | copy-start | bytes 6148
  113.9 59.8 %copy-start.2 = (f32[128]{0:T(128)S(1)}, f32[128]{0:T(128)}, u32[]{:S(2)}) copy-start(f32[128]{0:T(128)} %param.13) | copy-start | bytes 1540
Sparse Core Ops, SparseCore 0:
  9.2 29.3 all-gather.1
  137.9 35.7 reduce-scatter.1
where the time goes:
time: 183 us; the launch traced here: 182 us
  waiting for transfers between devices  67.2 us (37%)
  matrix products  54 us (30%)
  local copies, waits for them, and re-layouts  47 us (26%)
  between operations  14.1 us (8%)
    reduce_scatter x1, waiting for transfers between devices, local(): lax.psum_scatter(partial_value.astype(jnp.bfloat16), 'col', scatter_dimen...  35.9 us
    dot_general x1, local copies, waits for them, and re-layouts, local(): jnp.einsum('tij,tjf->tif', cell, picked, preferred_element_type=jnp.float32)  34.8 us
    all_gather x1, waiting for transfers between devices, local(): band = lax.all_gather(features, 'row', axis=0, tiled=True)  30.6 us
    dot_general x1, matrix products, local(): jnp.einsum('tij,tjf->tif', cell, picked, preferred_element_type=jnp.float32)  25.2 us
    dot_general x1, matrix products, local(): jnp.dot(row_select, prod.reshape(slots_n, 128 * width), precision=lax.Pre...  21.5 us
    unnamed x7, local copies, waits for them, and re-layouts  8.31 us
    dot_general x1, matrix products, local(): jnp.dot(col_select, band_flat, preferred_element_type=jnp.float32)  5.5 us
  transfers between devices with their start and end apart: 2, of which 2 were waited for; matrix products, arithmetic and copies ran while one was open for 0% of the time, Pallas kernels for 0%

commit v1 on v0

v1 whole, which is shorter than its diff:
```python
import functools

import jax
import jax.numpy as jnp
from jax import lax
from jax.experimental import pallas as pl
from jax.experimental.pallas import tpu as pltpu
from jax.sharding import PartitionSpec as P

MESH = pl.DeviceIdType.MESH
BLK = 128
GROUP = 16
CHUNK = 32
PIECES = 2


def gather_kernel(n_row, feat_ref, band_ref, send_sem, recv_sem, own_sem):
    me = lax.axis_index("row")
    own = feat_ref.shape[0]
    barrier = pltpu.get_barrier_semaphore()
    for k in range(1, n_row):
        peer = lax.rem(me + k, n_row)
        pl.semaphore_signal(barrier, inc=1, device_id={"row": peer}, device_id_type=MESH)
    pl.semaphore_wait(barrier, n_row - 1)
    slot = pl.ds(pl.multiple_of(me * own, own), own)
    copies = []
    for k in range(1, n_row):
        peer = lax.rem(me + k, n_row)
        copy = pltpu.make_async_remote_copy(
            src_ref=feat_ref,
            dst_ref=band_ref.at[slot],
            send_sem=send_sem.at[k],
            recv_sem=recv_sem.at[k],
            device_id={"row": peer},
            device_id_type=MESH,
        )
        copy.start()
        copies.append(copy)
    local_copy = pltpu.make_async_copy(feat_ref, band_ref.at[slot], own_sem)
    local_copy.start()
    local_copy.wait()
    for k in range(1, n_row):
        src = lax.rem(me - k + n_row, n_row)
        src_slot = pl.ds(pl.multiple_of(src * own, own), own)
        copies[k - 1].wait_send()
        pltpu.make_async_remote_copy(
            src_ref=feat_ref,
            dst_ref=band_ref.at[src_slot],
            send_sem=send_sem.at[k],
            recv_sem=recv_sem.at[k],
            device_id={"row": src},
            device_id_type=MESH,
        ).wait_recv()


def gather(features, n_row):
    own, width = features.shape
    return pl.pallas_call(
        functools.partial(gather_kernel, n_row),
        out_shape=jax.ShapeDtypeStruct((n_row * own, width), features.dtype),
        in_specs=[pl.BlockSpec(memory_space=pl.ANY)],
        out_specs=pl.BlockSpec(memory_space=pl.ANY),
        scratch_shapes=[
            pltpu.SemaphoreType.DMA((n_row,)),
            pltpu.SemaphoreType.DMA((n_row,)),
            pltpu.SemaphoreType.DMA,
        ],
        compiler_params=pltpu.CompilerParams(collective_id=0, has_side_effects=True),
        name="gather_band",
    )(features)


def cell_kernel(slots, row_blocks, rows_ref, cols_ref, count_ref, band_ref, tiles_ref, out_ref, held, acc, sem):
    count = count_ref[0]
    chunks = slots // CHUNK

    def chunk_copy(i):
        part = pl.ds(i * CHUNK, CHUNK)
        return pltpu.make_async_copy(tiles_ref.at[part], held.at[part], sem.at[i])

    for i in range(chunks):
        @pl.when(i * CHUNK < count)
        def _():
            chunk_copy(i).start()

    def clear(i, carry):
        acc[i] = jnp.zeros(acc.shape[1:], acc.dtype)
        return carry

    lax.fori_loop(0, row_blocks + 1, clear, 0, unroll=False)

    def group(g, carry):
        base = g * GROUP

        @pl.when(lax.rem(base, CHUNK) == 0)
        def _():
            chunk_copy(lax.div(base, CHUNK)).wait()

        for u in range(GROUP):
            t = base + u
            row = jnp.where(t < count, rows_ref[t], row_blocks)
            block = band_ref[cols_ref[t]]
            acc[row] += jnp.dot(held[t], block, preferred_element_type=jnp.float32)
        return carry

    lax.fori_loop(0, lax.div(count + GROUP - 1, GROUP), group, 0)

    def emit(i, carry):
        out_ref[i] = acc[i].astype(out_ref.dtype)
        return carry

    lax.fori_loop(0, row_blocks, emit, 0)


def cell_partial(rows, cols, count, band, tiles, row_blocks):
    slots = tiles.shape[0]
    width = band.shape[1]
    col_blocks = band.shape[0] // BLK
    smem = pl.BlockSpec(memory_space=pltpu.SMEM)
    vmem = pl.BlockSpec(memory_space=pltpu.VMEM)
    return pl.pallas_call(
        functools.partial(cell_kernel, slots, row_blocks),
        out_shape=jax.ShapeDtypeStruct((row_blocks, BLK, width), jnp.bfloat16),
        in_specs=[smem, smem, smem, vmem, pl.BlockSpec(memory_space=pl.ANY)],
        out_specs=vmem,
        scratch_shapes=[
            pltpu.VMEM((slots, BLK, BLK), jnp.bfloat16),
            pltpu.VMEM((row_blocks + 1, BLK, width), jnp.float32),
            pltpu.SemaphoreType.DMA((slots // CHUNK,)),
        ],
        compiler_params=pltpu.CompilerParams(vmem_limit_bytes=48 * 1024 * 1024),
        cost_estimate=pl.CostEstimate(
            flops=2 * slots * BLK * BLK * width, bytes_accessed=slots * BLK * BLK * 2, transcendentals=0
        ),
        name="cell_partial",
    )(rows, cols, count, band.reshape(col_blocks, BLK, width), tiles)


def reduce_kernel(
    line, own, part_ref, weight_ref, bias_ref, out_ref,
    pair_buf, up_in, down_in, up_out, down_out,
    pair_send, pair_recv, up_send, up_recv, down_send, down_recv,
):
    col = lax.axis_index("col")
    chip = lax.div(col, 2)
    core = lax.rem(col, 2)
    other = 1 - core
    rows = own // PIECES
    f32 = jnp.float32
    has_low = chip > 0
    has_high = chip < line - 1
    partner = chip * 2 + other
    high = lax.rem(col + 2, 2 * line)
    low = lax.rem(col - 2 + 2 * line, 2 * line)

    barrier = pltpu.get_barrier_semaphore()
    pl.semaphore_signal(barrier, inc=1, device_id={"col": partner}, device_id_type=MESH)

    @pl.when(has_low)
    def _():
        pl.semaphore_signal(barrier, inc=1, device_id={"col": low}, device_id_type=MESH)

    @pl.when(has_high)
    def _():
        pl.semaphore_signal(barrier, inc=1, device_id={"col": high}, device_id_type=MESH)

    pl.semaphore_wait(barrier, 1 + jnp.where(has_low, 1, 0) + jnp.where(has_high, 1, 0))

    def pair_copy(dest):
        start = pl.multiple_of((dest * 2 + other) * own, own)
        return pltpu.make_async_remote_copy(
            src_ref=part_ref.at[pl.ds(start, own)],
            dst_ref=pair_buf.at[dest],
            send_sem=pair_send.at[dest],
            recv_sem=pair_recv.at[dest],
            device_id={"col": partner},
            device_id_type=MESH,
        )

    def line_copy(dest, piece, upward):
        span = pl.ds(piece * rows, rows)
        src, dst = (up_out, up_in) if upward else (down_out, down_in)
        send, recv = (up_send, up_recv) if upward else (down_send, down_recv)
        return pltpu.make_async_remote_copy(
            src_ref=src.at[dest, span],
            dst_ref=dst.at[dest, span],
            send_sem=send.at[dest, piece],
            recv_sem=recv.at[dest, piece],
            device_id={"col": high if upward else low},
            device_id_type=MESH,
        )

    def pair_sum(dest, piece):
        mine = pl.ds(pl.multiple_of((dest * 2 + core) * own + piece * rows, rows), rows)
        span = pl.ds(piece * rows, rows)
        return part_ref[mine, :].astype(f32) + pair_buf[dest, span, :].astype(f32)

    for dist in range(line - 1, 0, -1):
        @pl.when(chip + dist < line)
        def _():
            pair_copy(chip + dist).start()

        @pl.when(chip - dist >= 0)
        def _():
            pair_copy(chip - dist).start()

    pair_copy(chip).start()

    def forward(dest, piece, upward):
        if piece == 0:
            pair_copy(dest).wait_recv()
        from_line = has_low if upward else has_high
        buf = up_in if upward else down_in
        out = up_out if upward else down_out
        span = pl.ds(piece * rows, rows)

        @pl.when(from_line)
        def _():
            line_copy(dest, piece, upward).wait_recv()
            out[dest, span, :] = (pair_sum(dest, piece) + buf[dest, span, :].astype(f32)).astype(out.dtype)

        @pl.when(jnp.logical_not(from_line))
        def _():
            out[dest, span, :] = pair_sum(dest, piece).astype(out.dtype)

        line_copy(dest, piece, upward).start()

    for dist in range(line - 1, 0, -1):
        for piece in range(PIECES):
            @pl.when(chip + dist < line)
            def _():
                forward(chip + dist, piece, True)

            @pl.when(chip - dist >= 0)
            def _():
                forward(chip - dist, piece, False)

    pair_copy(chip).wait_recv()
    for piece in range(PIECES):
        span = pl.ds(piece * rows, rows)

        @pl.when(has_low)
        def _():
            line_copy(chip, piece, True).wait_recv()

        @pl.when(has_high)
        def _():
            line_copy(chip, piece, False).wait_recv()

        total = pair_sum(chip, piece)
        total = total + jnp.where(has_low, up_in[chip, span, :].astype(f32), 0.0)
        total = total + jnp.where(has_high, down_in[chip, span, :].astype(f32), 0.0)
        mixed = jnp.dot(total.astype(jnp.bfloat16), weight_ref[...], preferred_element_type=f32)
        out_ref[span, :] = jnp.maximum(mixed + bias_ref[...], 0.0).astype(out_ref.dtype)

    for dest in range(line):
        pair_copy(dest).wait_send()
        for piece in range(PIECES):
            @pl.when(chip < dest)
            def _():
                line_copy(dest, piece, True).wait_send()

            @pl.when(chip > dest)
            def _():
                line_copy(dest, piece, False).wait_send()


def reduce_mix(partial_value, weight, bias, n_col, own):
    width = partial_value.shape[1]
    line = n_col // 2
    vmem = pl.BlockSpec(memory_space=pltpu.VMEM)
    buf = pltpu.VMEM((line, own, width), jnp.bfloat16)
    sems = pltpu.SemaphoreType.DMA((line, PIECES))
    pair_sems = pltpu.SemaphoreType.DMA((line,))
    return pl.pallas_call(
        functools.partial(reduce_kernel, line, own),
        out_shape=jax.ShapeDtypeStruct((own, width), jnp.bfloat16),
        in_specs=[vmem, vmem, vmem],
        out_specs=vmem,
        scratch_shapes=[buf, buf, buf, buf, buf, pair_sems, pair_sems, sems, sems, sems, sems],
        compiler_params=pltpu.CompilerParams(
            collective_id=1, has_side_effects=True, vmem_limit_bytes=48 * 1024 * 1024
        ),
        name="reduce_mix",
    )(partial_value, weight, bias)


def local(n_row, n_col, features, tiles, tile_rows, tile_cols, tile_counts, weight, bias):
    own, width = features.shape
    slots = tiles.shape[2]
    band = gather(features, n_row)
    row_blocks = n_col * own // BLK
    partial_value = cell_partial(
        tile_rows.reshape(slots),
        tile_cols.reshape(slots),
        tile_counts.reshape(1),
        band,
        tiles.reshape(slots, BLK, BLK),
        row_blocks,
    )
    return reduce_mix(
        partial_value.reshape(row_blocks * BLK, width), weight, bias.reshape(1, width), n_col, own
    )


def solution(mesh):
    in_specs = (
        P(("col", "row"), None),
        P("row", "col", None, None, None),
        P("row", "col", None),
        P("row", "col", None),
        P("row", "col"),
        P(),
        P(),
    )
    out_specs = P(("row", "col"), None)
    fn = functools.partial(local, mesh.shape["row"], mesh.shape["col"])
    return jax.shard_map(fn, mesh=mesh, in_specs=in_specs, out_specs=out_specs, check_vma=False)
```

time: 183 us -> 53.3 us (0.29)
  waiting for transfers between devices: 67.2 us -> 0 us
  matrix products: 54 us -> 0 us
  Pallas kernels: 0 us -> 48.9 us
  local copies, waits for them, and re-layouts: 47 us -> 3.29 us
  between operations: 14.1 us -> 0.72 us
    dot_general x4 -> x0, matrix products: 54 us -> none  [the longest x1 25.2 us: local(): jnp.einsum('tij,tjf->tif', cell, picked, preferred_element_type=jnp.float32)]
    pallas_call x0 -> x3, Pallas kernels: none -> 48.9 us  [the longest x1 20.3 us: reduce_mix(): pl.pallas_call(functools.partial(reduce_kernel, line, own), out_shape=jax...]
    reduce_scatter x1 -> x0, waiting for transfers between devices: 35.9 us -> none  [local(): lax.psum_scatter(partial_value.astype(jnp.bfloat16), 'col', scatter_dimen...]
    dot_general x1 -> x0, local copies, waits for them, and re-layouts: 34.8 us -> none  [local(): jnp.einsum('tij,tjf->tif', cell, picked, preferred_element_type=jnp.float32)]
    all_gather x1 -> x0, waiting for transfers between devices: 30.6 us -> none  [local(): band = lax.all_gather(features, 'row', axis=0, tiled=True)]
    unnamed x7 -> x11, local copies, waits for them, and re-layouts: 8.31 us -> 3.29 us
    convert_element_type x1 -> x0, local copies, waits for them, and re-layouts: 2.36 us -> none  [local(): partial_value.astype(jnp.bfloat16)]
  transfers between devices with their start and end apart: 2 -> 0, of which waited for: 2 -> 0; matrix products, arithmetic and copies ran while one was open for 0% -> 0% of each run, Pallas kernels for 0% -> 0%
where the time goes in v1:
time: 53.3 us; the launch traced here: 52.9 us
  Pallas kernels  48.9 us (92%)
  local copies, waits for them, and re-layouts  3.29 us (6%)
  between operations  0.72 us (1%)
    pallas_call x1, Pallas kernels, reduce_mix(): pl.pallas_call(functools.partial(reduce_kernel, line, own), out_shape=jax...  20.3 us
    pallas_call x1, Pallas kernels, gather(): pl.pallas_call(functools.partial(gather_kernel, n_row), out_shape=jax.Sha...  16.6 us
    pallas_call x1, Pallas kernels, cell_partial(): pl.pallas_call(functools.partial(cell_kernel, slots, row_blocks), out_sha...  12 us
    unnamed x11, local copies, waits for them, and re-layouts  3.29 us

profile of v1, /device:TPU:0, one launch (start us, length us, event | category | flops | bytes accessed | tf_op | source)
XLA Modules:
  0.0 52.9 jit_solution(1138826919108615834)
XLA Ops:
  0.0 0.0 copy-start.4
  0.0 0.0 copy-start.1
  0.7 16.6 %gather_band.1 = bf16[4096,128]{1,0:T(8,128)(2,1)} custom-call(bf16[1024,128]{1,0:T(8,128)(2,1)} %feat_ref.1), custom_call_target="tpu_custom_call" | custom-call | tf_op jit(solution)/shard_map/gather_band/pallas_call | solution.py:58
  17.3 0.0 copy-start
  17.3 1.2 %copy-done = bf16[4096,128]{1,0:T(8,128)(2,1)S(1)} copy-done((bf16[4096,128]{1,0:T(8,128)(2,1)S(1)}, bf16[4096,128]{1,0:T(8,128)(2,1)}, u32[]{:S(2)}) %copy-start) | copy-done | bytes 1048600
  18.5 0.0 copy-start.2
  18.5 0.7 %copy-done.2 = s32[1,1,512]{2,1,0:T(1,128)S(1)} copy-done((s32[1,1,512]{2,1,0:T(1,128)S(1)}, s32[1,1,512]{2,1,0:T(1,128)}, u32[]{:S(2)}) %copy-start.2) | copy-done | bytes 2072
  19.2 0.0 copy-start.3
  19.2 0.7 %copy-done.3 = s32[1,1,512]{2,1,0:T(1,128)S(1)} copy-done((s32[1,1,512]{2,1,0:T(1,128)S(1)}, s32[1,1,512]{2,1,0:T(1,128)}, u32[]{:S(2)}) %copy-start.3) | copy-done | bytes 2072
  19.9 12.0 %cell_partial.1 = bf16[64,128,128]{2,1,0:T(8,128)(2,1)S(1)} custom-call(s32[512]{0:T(512)S(1)} %bitcast.10, s32[512]{0:T(512)S(1)} %bitcast.11, s32[1]{0:T(128)} %bitcast.7.count_ref, bf16[32,128,128]{2,1,0:T(8,128)(2,1)S(1)} %bitcast.9, bf16[512,128,128]{2,1,0:T(8,128)(2,1)} %bitcast.13), custom_call_target="tpu_custom_call" | custom-call | flops 2147483648 | bytes 16777216 | tf_op jit(solution)/shard_map/cell_partial/pallas_call | solution.py:121
  31.9 0.0 copy-done.4
  31.9 0.0 copy-done.1
  31.9 20.3 %reduce_mix.1 = bf16[1024,128]{1,0:T(8,128)(2,1)S(1)} custom-call(bf16[8192,128]{1,0:T(8,128)(2,1)S(1)} %bitcast.8, bf16[128,128]{1,0:T(8,128)(2,1)S(1)} %copy-done.1, f32[1,128]{1,0:T(1,128)S(1)} %bitcast.12), custom_call_target="tpu_custom_call" | custom-call | tf_op jit(solution)/shard_map/reduce_mix/pallas_call | solution.py:275
  52.2 0.7 %copy.10 = bf16[1024,128]{1,0:T(8,128)(2,1)} copy(bf16[1024,128]{1,0:T(8,128)(2,1)S(1)} %reduce_mix.1) | data formatting | bytes 524288
Async XLA Ops:
  0.0 31.9 %copy-start.4 = (f32[128]{0:T(128)S(1)}, f32[128]{0:T(128)}, u32[]{:S(2)}) copy-start(f32[128]{0:T(128)} %param.13) | copy-start | bytes 1540
  0.0 31.9 %copy-start.1 = (bf16[128,128]{1,0:T(8,128)(2,1)S(1)}, bf16[128,128]{1,0:T(8,128)(2,1)}, u32[]{:S(2)}) copy-start(bf16[128,128]{1,0:T(8,128)(2,1)} %weight_ref.1) | copy-start | bytes 98308
  17.3 1.2 %copy-start = (bf16[4096,128]{1,0:T(8,128)(2,1)S(1)}, bf16[4096,128]{1,0:T(8,128)(2,1)}, u32[]{:S(2)}) copy-start(bf16[4096,128]{1,0:T(8,128)(2,1)} %gather_band.1) | copy-start | bytes 3145732
  18.5 0.7 %copy-start.2 = (s32[1,1,512]{2,1,0:T(1,128)S(1)}, s32[1,1,512]{2,1,0:T(1,128)}, u32[]{:S(2)}) copy-start(s32[1,1,512]{2,1,0:T(1,128)} %param.9) | copy-start | bytes 6148
  19.2 0.7 %copy-start.3 = (s32[1,1,512]{2,1,0:T(1,128)S(1)}, s32[1,1,512]{2,1,0:T(1,128)}, u32[]{:S(2)}) copy-start(s32[1,1,512]{2,1,0:T(1,128)} %param.10) | copy-start | bytes 6148

commit v2 on v1

--- a/solution.py
+++ b/solution.py
@@ -9,9 +9,8 @@
 
 MESH = pl.DeviceIdType.MESH
 BLK = 128
-GROUP = 16
 CHUNK = 32
-PIECES = 2
+PIECES = 4
 
 
 def gather_kernel(n_row, feat_ref, band_ref, send_sem, recv_sem, own_sem):
@@ -53,24 +52,80 @@
         ).wait_recv()
 
 
+def relay_kernel(feat_ref, band_ref, send_sem, recv_sem, own_sem):
+    me = lax.axis_index("row")
+    own = feat_ref.shape[0]
+    half = own // 2
+    slow, fast = lax.div(me, 2), lax.rem(me, 2)
+    peers = (slow * 2 + (1 - fast), (1 - slow) * 2 + fast)
+    opposite = (1 - slow) * 2 + (1 - fast)
+    barrier = pltpu.get_barrier_semaphore()
+    for peer in peers:
+        pl.semaphore_signal(barrier, inc=1, device_id={"row": peer}, device_id_type=MESH)
+    local_copy = pltpu.make_async_copy(feat_ref, band_ref.at[pl.ds(pl.multiple_of(me * own, own), own)], own_sem)
+    local_copy.start()
+    pl.semaphore_wait(barrier, 2)
+
+    def span(owner, part):
+        return pl.ds(pl.multiple_of(owner * own + part * half, half), half)
+
+    def copy(axis, step, source, owner, part):
+        return pltpu.make_async_remote_copy(
+            src_ref=source,
+            dst_ref=band_ref.at[span(owner, part)],
+            send_sem=send_sem.at[axis, step],
+            recv_sem=recv_sem.at[axis, step],
+            device_id={"row": peers[axis]},
+            device_id_type=MESH,
+        )
+
+    def own_part(part):
+        return feat_ref.at[pl.ds(part * half, half)]
+
+    for step in range(2):
+        for axis in range(2):
+            part = axis if step == 0 else 1 - axis
+            copy(axis, step, own_part(part), me, part).start()
+    for axis in range(2):
+        copy(axis, 0, own_part(axis), peers[axis], axis).wait_recv()
+        copy(1 - axis, 2, band_ref.at[span(peers[axis], axis)], peers[axis], axis).start()
+    local_copy.wait()
+    for axis in range(2):
+        copy(axis, 1, own_part(0), peers[axis], 1 - axis).wait_recv()
+    for axis in range(2):
+        copy(axis, 2, own_part(0), opposite, 1 - axis).wait_recv()
+    for axis in range(2):
+        for step in range(3):
+            copy(axis, step, own_part(0), me, 0).wait_send()
+
+
 def gather(features, n_row):
     own, width = features.shape
+    if n_row == 4:
+        kernel, sem_shape = relay_kernel, (2, 3)
+    else:
+        kernel, sem_shape = functools.partial(gather_kernel, n_row), (n_row,)
     return pl.pallas_call(
-        functools.partial(gather_kernel, n_row),
+        kernel,
         out_shape=jax.ShapeDtypeStruct((n_row * own, width), features.dtype),
         in_specs=[pl.BlockSpec(memory_space=pl.ANY)],
-        out_specs=pl.BlockSpec(memory_space=pl.ANY),
+        out_specs=pl.BlockSpec(memory_space=pltpu.VMEM),
         scratch_shapes=[
-            pltpu.SemaphoreType.DMA((n_row,)),
-            pltpu.SemaphoreType.DMA((n_row,)),
+            pltpu.SemaphoreType.DMA(sem_shape),
+            pltpu.SemaphoreType.DMA(sem_shape),
             pltpu.SemaphoreType.DMA,
         ],
-        compiler_params=pltpu.CompilerParams(collective_id=0, has_side_effects=True),
+        compiler_params=pltpu.CompilerParams(
+            collective_id=0, has_side_effects=True, vmem_limit_bytes=16 * 1024 * 1024
+        ),
         name="gather_band",
     )(features)
 
 
-def cell_kernel(slots, row_blocks, rows_ref, cols_ref, count_ref, band_ref, tiles_ref, out_ref, held, acc, sem):
+def cell_kernel(
+    slots, row_blocks, rows_hbm, cols_hbm, count_ref, band_ref, tiles_ref, out_ref,
+    rows_ref, cols_ref, held, acc, sem, index_sem,
+):
     count = count_ref[0]
     chunks = slots // CHUNK
 
@@ -78,6 +133,10 @@
         part = pl.ds(i * CHUNK, CHUNK)
         return pltpu.make_async_copy(tiles_ref.at[part], held.at[part], sem.at[i])
 
+    rows_copy = pltpu.make_async_copy(rows_hbm, rows_ref, index_sem.at[0])
+    cols_copy = pltpu.make_async_copy(cols_hbm, cols_ref, index_sem.at[1])
+    rows_copy.start()
+    cols_copy.start()
     for i in range(chunks):
         @pl.when(i * CHUNK < count)
         def _():
@@ -87,29 +146,26 @@
         acc[i] = jnp.zeros(acc.shape[1:], acc.dtype)
         return carry
 
-    lax.fori_loop(0, row_blocks + 1, clear, 0, unroll=False)
-
-    def group(g, carry):
-        base = g * GROUP
-
-        @pl.when(lax.rem(base, CHUNK) == 0)
-        def _():
-            chunk_copy(lax.div(base, CHUNK)).wait()
-
-        for u in range(GROUP):
-            t = base + u
+    lax.fori_loop(0, row_blocks, clear, 0, unroll=8)
+    rows_copy.wait()
+    cols_copy.wait()
+
+    def chunk_step(i, carry):
+        chunk_copy(i).wait()
+        for u in range(CHUNK):
+            t = i * CHUNK + u
             row = jnp.where(t < count, rows_ref[t], row_blocks)
             block = band_ref[cols_ref[t]]
             acc[row] += jnp.dot(held[t], block, preferred_element_type=jnp.float32)
         return carry
 
-    lax.fori_loop(0, lax.div(count + GROUP - 1, GROUP), group, 0)
+    lax.fori_loop(0, lax.div(count + CHUNK - 1, CHUNK), chunk_step, 0)
 
     def emit(i, carry):
         out_ref[i] = acc[i].astype(out_ref.dtype)
         return carry
 
-    lax.fori_loop(0, row_blocks, emit, 0)
+    lax.fori_loop(0, row_blocks, emit, 0, unroll=8)
 
 
 def cell_partial(rows, cols, count, band, tiles, row_blocks):
@@ -117,16 +173,20 @@
     width = band.shape[1]
     col_blocks = band.shape[0] // BLK
     smem = pl.BlockSpec(memory_space=pltpu.SMEM)
+    hbm = pl.BlockSpec(memory_space=pl.ANY)
     vmem = pl.BlockSpec(memory_space=pltpu.VMEM)
     return pl.pallas_call(
         functools.partial(cell_kernel, slots, row_blocks),
         out_shape=jax.ShapeDtypeStruct((row_blocks, BLK, width), jnp.bfloat16),
-        in_specs=[smem, smem, smem, vmem, pl.BlockSpec(memory_space=pl.ANY)],
+        in_specs=[hbm, hbm, smem, vmem, hbm],
         out_specs=vmem,
         scratch_shapes=[
+            pltpu.SMEM((slots,), jnp.int32),
+            pltpu.SMEM((slots,), jnp.int32),
             pltpu.VMEM((slots, BLK, BLK), jnp.bfloat16),
             pltpu.VMEM((row_blocks + 1, BLK, width), jnp.float32),
             pltpu.SemaphoreType.DMA((slots // CHUNK,)),
+            pltpu.SemaphoreType.DMA((2,)),
         ],
         compiler_params=pltpu.CompilerParams(vmem_limit_bytes=48 * 1024 * 1024),
         cost_estimate=pl.CostEstimate(

time: 53.3 us -> 46.3 us (0.87)
  Pallas kernels: 48.9 us -> 42.7 us
    pallas_call x1, Pallas kernels: 16.6 us -> 13.4 us  [gather(): pl.pallas_call(kernel, out_shape=jax.ShapeDtypeStruct((n_row * own, width...]
    pallas_call x1, Pallas kernels: 12 us -> 9.3 us  [cell_partial(): pl.pallas_call(functools.partial(cell_kernel, slots, row_blocks), out_sha...]
where the time goes in v2:
time: 46.3 us; the launch traced here: 46.4 us
  Pallas kernels  42.7 us (92%)
  local copies, waits for them, and re-layouts  3.01 us (7%)
  between operations  0.73 us (2%)
    pallas_call x1, Pallas kernels, reduce_mix(): pl.pallas_call(functools.partial(reduce_kernel, line, own), out_shape=jax...  20 us
    pallas_call x1, Pallas kernels, gather(): pl.pallas_call(kernel, out_shape=jax.ShapeDtypeStruct((n_row * own, width...  13.4 us
    pallas_call x1, Pallas kernels, cell_partial(): pl.pallas_call(functools.partial(cell_kernel, slots, row_blocks), out_sha...  9.3 us
    unnamed x11, local copies, waits for them, and re-layouts  3.01 us

profile of v2, /device:TPU:0, one launch (start us, length us, event | category | flops | bytes accessed | tf_op | source)
XLA Modules:
  0.0 46.4 jit_solution(13884365126383723998)
XLA Ops:
  0.0 0.0 copy-start.4
  0.7 0.0 copy-start
  0.7 0.9 %copy-done = bf16[1024,128]{1,0:T(8,128)(2,1)S(1)} copy-done((bf16[1024,128]{1,0:T(8,128)(2,1)S(1)}, bf16[1024,128]{1,0:T(8,128)(2,1)}, u32[]{:S(2)}) %copy-start) | copy-done | bytes 262168
  1.6 0.0 copy-start.1
  1.6 13.4 %gather_band.1 = bf16[4096,128]{1,0:T(8,128)(2,1)S(1)} custom-call(bf16[1024,128]{1,0:T(8,128)(2,1)S(1)} %copy-done), custom_call_target="tpu_custom_call" | custom-call | tf_op jit(solution)/shard_map/gather_band/pallas_call | solution.py:108
  15.0 0.0 copy-start.2
  15.1 0.7 %copy-done.2 = s32[1,1,512]{2,1,0:T(1,128)S(1)} copy-done((s32[1,1,512]{2,1,0:T(1,128)S(1)}, s32[1,1,512]{2,1,0:T(1,128)}, u32[]{:S(2)}) %copy-start.2) | copy-done | bytes 2072
  15.7 0.0 copy-start.3
  15.7 0.7 %copy-done.3 = s32[1,1,512]{2,1,0:T(1,128)S(1)} copy-done((s32[1,1,512]{2,1,0:T(1,128)S(1)}, s32[1,1,512]{2,1,0:T(1,128)}, u32[]{:S(2)}) %copy-start.3) | copy-done | bytes 2072
  16.4 9.3 %cell_partial.1 = bf16[64,128,128]{2,1,0:T(8,128)(2,1)S(1)} custom-call(s32[512]{0:T(512)S(1)} %bitcast.10, s32[512]{0:T(512)S(1)} %bitcast.11, s32[1]{0:T(128)} %bitcast.7.count_ref, bf16[32,128,128]{2,1,0:T(8,128)(2,1)S(1)} %bitcast.9, bf16[512,128,128]{2,1,0:T(8,128)(2,1)} %bitcast.13), custom_call_target="tpu_custom_call" | custom-call | flops 2147483648 | bytes 16777216 | tf_op jit(solution)/shard_map/cell_partial/pallas_call | solution.py:178
  25.7 0.0 copy-done.4
  25.7 0.0 copy-done.1
  25.7 20.0 %reduce_mix.1 = bf16[1024,128]{1,0:T(8,128)(2,1)S(1)} custom-call(bf16[8192,128]{1,0:T(8,128)(2,1)S(1)} %bitcast.8, bf16[128,128]{1,0:T(8,128)(2,1)S(1)} %copy-done.1, f32[1,128]{1,0:T(1,128)S(1)} %bitcast.12), custom_call_target="tpu_custom_call" | custom-call | tf_op jit(solution)/shard_map/reduce_mix/pallas_call | solution.py:335
  45.7 0.7 %copy.10 = bf16[1024,128]{1,0:T(8,128)(2,1)} copy(bf16[1024,128]{1,0:T(8,128)(2,1)S(1)} %reduce_mix.1) | data formatting | bytes 524288
Async XLA Ops:
  0.0 25.7 %copy-start.4 = (f32[128]{0:T(128)S(1)}, f32[128]{0:T(128)}, u32[]{:S(2)}) copy-start(f32[128]{0:T(128)} %param.13) | copy-start | bytes 1540
  0.7 1.0 %copy-start = (bf16[1024,128]{1,0:T(8,128)(2,1)S(1)}, bf16[1024,128]{1,0:T(8,128)(2,1)}, u32[]{:S(2)}) copy-start(bf16[1024,128]{1,0:T(8,128)(2,1)} %feat_ref.1) | copy-start | bytes 786436
  1.6 24.1 %copy-start.1 = (bf16[128,128]{1,0:T(8,128)(2,1)S(1)}, bf16[128,128]{1,0:T(8,128)(2,1)}, u32[]{:S(2)}) copy-start(bf16[128,128]{1,0:T(8,128)(2,1)} %weight_ref.1) | copy-start | bytes 98308
  15.0 0.7 %copy-start.2 = (s32[1,1,512]{2,1,0:T(1,128)S(1)}, s32[1,1,512]{2,1,0:T(1,128)}, u32[]{:S(2)}) copy-start(s32[1,1,512]{2,1,0:T(1,128)} %param.9) | copy-start | bytes 6148
  15.7 0.7 %copy-start.3 = (s32[1,1,512]{2,1,0:T(1,128)S(1)}, s32[1,1,512]{2,1,0:T(1,128)}, u32[]{:S(2)}) copy-start(s32[1,1,512]{2,1,0:T(1,128)} %param.10) | copy-start | bytes 6148

commit v3 on v2

--- a/solution.py
+++ b/solution.py
@@ -9,11 +9,19 @@
 
 MESH = pl.DeviceIdType.MESH
 BLK = 128
-CHUNK = 32
+CHUNK = 64
 PIECES = 4
 
 
-def gather_kernel(n_row, feat_ref, band_ref, send_sem, recv_sem, own_sem):
+def fill_zero(total_ref):
+    def fill(i, carry):
+        total_ref[i] = jnp.zeros(total_ref.shape[1:], total_ref.dtype)
+        return carry
+
+    lax.fori_loop(0, total_ref.shape[0], fill, 0)
+
+
+def gather_kernel(n_row, feat_ref, band_ref, total_ref, send_sem, recv_sem, own_sem):
     me = lax.axis_index("row")
     own = feat_ref.shape[0]
     barrier = pltpu.get_barrier_semaphore()
@@ -37,6 +45,7 @@
         copies.append(copy)
     local_copy = pltpu.make_async_copy(feat_ref, band_ref.at[slot], own_sem)
     local_copy.start()
+    fill_zero(total_ref)
     local_copy.wait()
     for k in range(1, n_row):
         src = lax.rem(me - k + n_row, n_row)
@@ -52,7 +61,7 @@
         ).wait_recv()
 
 
-def relay_kernel(feat_ref, band_ref, send_sem, recv_sem, own_sem):
+def relay_kernel(feat_ref, band_ref, total_ref, send_sem, recv_sem, own_sem):
     me = lax.axis_index("row")
     own = feat_ref.shape[0]
     half = own // 2
@@ -86,6 +95,7 @@
         for axis in range(2):
             part = axis if step == 0 else 1 - axis
             copy(axis, step, own_part(part), me, part).start()
+    fill_zero(total_ref)
     for axis in range(2):
         copy(axis, 0, own_part(axis), peers[axis], axis).wait_recv()
         copy(1 - axis, 2, band_ref.at[span(peers[axis], axis)], peers[axis], axis).start()
@@ -99,7 +109,7 @@
             copy(axis, step, own_part(0), me, 0).wait_send()
 
 
-def gather(features, n_row):
+def gather(features, n_row, row_blocks):
     own, width = features.shape
     if n_row == 4:
         kernel, sem_shape = relay_kernel, (2, 3)
@@ -107,9 +117,12 @@
         kernel, sem_shape = functools.partial(gather_kernel, n_row), (n_row,)
     return pl.pallas_call(
         kernel,
-        out_shape=jax.ShapeDtypeStruct((n_row * own, width), features.dtype),
+        out_shape=(
+            jax.ShapeDtypeStruct((n_row * own, width), features.dtype),
+            jax.ShapeDtypeStruct((row_blocks + 1, BLK, width), jnp.float32),
+        ),
         in_specs=[pl.BlockSpec(memory_space=pl.ANY)],
-        out_specs=pl.BlockSpec(memory_space=pltpu.VMEM),
+        out_specs=(pl.BlockSpec(memory_space=pltpu.VMEM), pl.BlockSpec(memory_space=pltpu.VMEM)),
         scratch_shapes=[
             pltpu.SemaphoreType.DMA(sem_shape),
             pltpu.SemaphoreType.DMA(sem_shape),
@@ -122,83 +135,69 @@
     )(features)
 
 
-def cell_kernel(
-    slots, row_blocks, rows_hbm, cols_hbm, count_ref, band_ref, tiles_ref, out_ref,
-    rows_ref, cols_ref, held, acc, sem, index_sem,
-):
-    count = count_ref[0]
+def cell_kernel(slots, index_hbm, band_ref, tiles_ref, zero_ref, acc, index_ref, held, sem, index_sem):
     chunks = slots // CHUNK
+    first = min(max(128 // CHUNK, 1), chunks)
 
     def chunk_copy(i):
         part = pl.ds(i * CHUNK, CHUNK)
         return pltpu.make_async_copy(tiles_ref.at[part], held.at[part], sem.at[i])
 
-    rows_copy = pltpu.make_async_copy(rows_hbm, rows_ref, index_sem.at[0])
-    cols_copy = pltpu.make_async_copy(cols_hbm, cols_ref, index_sem.at[1])
-    rows_copy.start()
-    cols_copy.start()
-    for i in range(chunks):
+    index_copy = pltpu.make_async_copy(index_hbm, index_ref, index_sem)
+    index_copy.start()
+    for i in range(first):
+        chunk_copy(i).start()
+    index_copy.wait()
+    count = index_ref[slots]
+    for i in range(first, chunks):
         @pl.when(i * CHUNK < count)
         def _():
             chunk_copy(i).start()
-
-    def clear(i, carry):
-        acc[i] = jnp.zeros(acc.shape[1:], acc.dtype)
-        return carry
-
-    lax.fori_loop(0, row_blocks, clear, 0, unroll=8)
-    rows_copy.wait()
-    cols_copy.wait()
 
     def chunk_step(i, carry):
         chunk_copy(i).wait()
         for u in range(CHUNK):
             t = i * CHUNK + u
-            row = jnp.where(t < count, rows_ref[t], row_blocks)
-            block = band_ref[cols_ref[t]]
-            acc[row] += jnp.dot(held[t], block, preferred_element_type=jnp.float32)
+            index = index_ref[t]
+            block = band_ref[index & 0xFFFF]
+            acc[index >> 16] += jnp.dot(held[t], block, preferred_element_type=jnp.float32)
         return carry
 
-    lax.fori_loop(0, lax.div(count + CHUNK - 1, CHUNK), chunk_step, 0)
-
-    def emit(i, carry):
-        out_ref[i] = acc[i].astype(out_ref.dtype)
-        return carry
-
-    lax.fori_loop(0, row_blocks, emit, 0, unroll=8)
-
-
-def cell_partial(rows, cols, count, band, tiles, row_blocks):
+    lax.fori_loop(0, jnp.maximum(lax.div(count + CHUNK - 1, CHUNK), first), chunk_step, 0)
+
+
+def cell_partial(rows, cols, count, band, tiles, zero):
     slots = tiles.shape[0]
     width = band.shape[1]
     col_blocks = band.shape[0] // BLK
-    smem = pl.BlockSpec(memory_space=pltpu.SMEM)
+    row_blocks = zero.shape[0] - 1
+    live_rows = jnp.where(jnp.arange(slots, dtype=jnp.int32) < count, rows, row_blocks)
+    index = jnp.concatenate([live_rows * 65536 + cols, jnp.broadcast_to(count, (BLK,))])
     hbm = pl.BlockSpec(memory_space=pl.ANY)
     vmem = pl.BlockSpec(memory_space=pltpu.VMEM)
     return pl.pallas_call(
-        functools.partial(cell_kernel, slots, row_blocks),
-        out_shape=jax.ShapeDtypeStruct((row_blocks, BLK, width), jnp.bfloat16),
-        in_specs=[hbm, hbm, smem, vmem, hbm],
+        functools.partial(cell_kernel, slots),
+        out_shape=jax.ShapeDtypeStruct(zero.shape, zero.dtype),
+        in_specs=[hbm, vmem, hbm, vmem],
         out_specs=vmem,
         scratch_shapes=[
-            pltpu.SMEM((slots,), jnp.int32),
-            pltpu.SMEM((slots,), jnp.int32),
+            pltpu.SMEM((slots + BLK,), jnp.int32),
             pltpu.VMEM((slots, BLK, BLK), jnp.bfloat16),
-            pltpu.VMEM((row_blocks + 1, BLK, width), jnp.float32),
             pltpu.SemaphoreType.DMA((slots // CHUNK,)),
-            pltpu.SemaphoreType.DMA((2,)),
+            pltpu.SemaphoreType.DMA,
         ],
+        input_output_aliases={3: 0},
         compiler_params=pltpu.CompilerParams(vmem_limit_bytes=48 * 1024 * 1024),
         cost_estimate=pl.CostEstimate(
             flops=2 * slots * BLK * BLK * width, bytes_accessed=slots * BLK * BLK * 2, transcendentals=0
         ),
         name="cell_partial",
-    )(rows, cols, count, band.reshape(col_blocks, BLK, width), tiles)
+    )(index, band.reshape(col_blocks, BLK, width), tiles, zero)
 
 
 def reduce_kernel(
     line, own, part_ref, weight_ref, bias_ref, out_ref,
-    pair_buf, up_in, down_in, up_out, down_out,
+    pair_out, pair_buf, up_in, down_in, up_out, down_out,
     pair_send, pair_recv, up_send, up_recv, down_send, down_recv,
 ):
     col = lax.axis_index("col")
@@ -226,16 +225,22 @@
 
     pl.semaphore_wait(barrier, 1 + jnp.where(has_low, 1, 0) + jnp.where(has_high, 1, 0))
 
-    def pair_copy(dest):
-        start = pl.multiple_of((dest * 2 + other) * own, own)
+    def pair_copy(dest, piece):
+        span = pl.ds(piece * rows, rows)
         return pltpu.make_async_remote_copy(
-            src_ref=part_ref.at[pl.ds(start, own)],
-            dst_ref=pair_buf.at[dest],
-            send_sem=pair_send.at[dest],
-            recv_sem=pair_recv.at[dest],
+            src_ref=pair_out.at[dest, span],
+            dst_ref=pair_buf.at[dest, span],
+            send_sem=pair_send.at[dest, piece],
+            recv_sem=pair_recv.at[dest, piece],
             device_id={"col": partner},
             device_id_type=MESH,
         )
+
+    def pair_start(dest):
+        for piece in range(PIECES):
+            theirs = pl.ds(pl.multiple_of((dest * 2 + other) * own + piece * rows, rows), rows)
+            pair_out[dest, pl.ds(piece * rows, rows), :] = part_ref[theirs, :].astype(pair_out.dtype)
+            pair_copy(dest, piece).start()
 
     def line_copy(dest, piece, upward):
         span = pl.ds(piece * rows, rows)
@@ -253,22 +258,21 @@
     def pair_sum(dest, piece):
         mine = pl.ds(pl.multiple_of((dest * 2 + core) * own + piece * rows, rows), rows)
         span = pl.ds(piece * rows, rows)
-        return part_ref[mine, :].astype(f32) + pair_buf[dest, span, :].astype(f32)
+        return part_ref[mine, :] + pair_buf[dest, span, :].astype(f32)
 
     for dist in range(line - 1, 0, -1):
         @pl.when(chip + dist < line)
         def _():
-            pair_copy(chip + dist).start()
+            pair_start(chip + dist)
 
         @pl.when(chip - dist >= 0)
         def _():
-            pair_copy(chip - dist).start()
-
-    pair_copy(chip).start()
+            pair_start(chip - dist)
+
+    pair_start(chip)
 
     def forward(dest, piece, upward):
-        if piece == 0:
-            pair_copy(dest).wait_recv()
+        pair_copy(dest, piece).wait_recv()
         from_line = has_low if upward else has_high
         buf = up_in if upward else down_in
         out = up_out if upward else down_out
@@ -295,9 +299,9 @@
             def _():
                 forward(chip - dist, piece, False)
 
-    pair_copy(chip).wait_recv()
     for piece in range(PIECES):
         span = pl.ds(piece * rows, rows)
+        pair_copy(chip, piece).wait_recv()
 
         @pl.when(has_low)
         def _():
@@ -314,8 +318,9 @@
         out_ref[span, :] = jnp.maximum(mixed + bias_ref[...], 0.0).astype(out_ref.dtype)
 
     for dest in range(line):
-        pair_copy(dest).wait_send()
         for piece in range(PIECES):
+            pair_copy(dest, piece).wait_send()
+
             @pl.when(chip < dest)
             def _():
                 line_copy(dest, piece, True).wait_send()
@@ -331,15 +336,14 @@
     vmem = pl.BlockSpec(memory_space=pltpu.VMEM)
     buf = pltpu.VMEM((line, own, width), jnp.bfloat16)
     sems = pltpu.SemaphoreType.DMA((line, PIECES))
-    pair_sems = pltpu.SemaphoreType.DMA((line,))
     return pl.pallas_call(
         functools.partial(reduce_kernel, line, own),
         out_shape=jax.ShapeDtypeStruct((own, width), jnp.bfloat16),
         in_specs=[vmem, vmem, vmem],
         out_specs=vmem,
-        scratch_shapes=[buf, buf, buf, buf, buf, pair_sems, pair_sems, sems, sems, sems, sems],
+        scratch_shapes=[buf] * 6 + [sems] * 6,
         compiler_params=pltpu.CompilerParams(
-            collective_id=1, has_side_effects=True, vmem_limit_bytes=48 * 1024 * 1024
+            collective_id=1, has_side_effects=True, vmem_limit_bytes=32 * 1024 * 1024
         ),
         name="reduce_mix",
     )(partial_value, weight, bias)
@@ -348,18 +352,18 @@
 def local(n_row, n_col, features, tiles, tile_rows, tile_cols, tile_counts, weight, bias):
     own, width = features.shape
     slots = tiles.shape[2]
-    band = gather(features, n_row)
     row_blocks = n_col * own // BLK
+    band, zero = gather(features, n_row, row_blocks)
     partial_value = cell_partial(
         tile_rows.reshape(slots),
         tile_cols.reshape(slots),
         tile_counts.reshape(1),
         band,
         tiles.reshape(slots, BLK, BLK),
-        row_blocks,
+        zero,
     )
     return reduce_mix(
-        partial_value.reshape(row_blocks * BLK, width), weight, bias.reshape(1, width), n_col, own
+        partial_value.reshape((row_blocks + 1) * BLK, width), weight, bias.reshape(1, width), n_col, own
     )
 
 

time: 46.3 us -> 45.4 us (0.981)
  the two profiles are of different devices: /device:TPU:0 before, /device:TPU:17 now
where the time goes in v3:
time: 45.4 us; the launch traced here: 45.2 us
  Pallas kernels  42.1 us (93%)
  local copies, waits for them, and re-layouts  1.67 us (4%)
  other arithmetic  0.71 us (2%)
  between operations  0.71 us (2%)
    pallas_call x1, Pallas kernels, reduce_mix(): pl.pallas_call(functools.partial(reduce_kernel, line, own), out_shape=jax...  22.6 us
    pallas_call x1, Pallas kernels, gather(): pl.pallas_call(kernel, out_shape=(jax.ShapeDtypeStruct((n_row * own, widt...  11.1 us
    pallas_call x1, Pallas kernels, cell_partial(): pl.pallas_call(functools.partial(cell_kernel, slots), out_shape=jax.Shape...  8.41 us
    unnamed x7, local copies, waits for them, and re-layouts  1.67 us

profile of v3, /device:TPU:17, one launch (start us, length us, event | category | flops | bytes accessed | tf_op | source)
XLA Modules:
  0.0 45.2 jit_solution(9739226019832091451)
XLA Ops:
  0.7 0.7 %multiply_add_fusion = s32[512]{0:T(512)S(1)} fusion(s32[512]{0:T(512)} %bitcast.13, s32[512]{0:T(512)} %bitcast.14, s32[]{:T(128)} %bitcast.7), kind=kLoop, calls=%fused_computation | loop fusion | flops 2048 | bytes 6148 | tf_op jit(solution)/shard_map/add | solution.py:175
  1.4 0.0 copy-start
  1.4 0.9 %copy-done = bf16[1024,128]{1,0:T(8,128)(2,1)S(1)} copy-done((bf16[1024,128]{1,0:T(8,128)(2,1)S(1)}, bf16[1024,128]{1,0:T(8,128)(2,1)}, u32[]{:S(2)}) %copy-start) | copy-done | bytes 262168
  2.3 11.1 %gather_band.1 = (bf16[4096,128]{1,0:T(8,128)(2,1)S(1)}, f32[65,128,128]{2,1,0:T(8,128)S(1)}) custom-call(bf16[1024,128]{1,0:T(8,128)(2,1)S(1)} %copy-done), custom_call_target="tpu_custom_call" | custom-call | tf_op jit(solution)/shard_map/gather_band/pallas_call | solution.py:118
  13.4 0.0 copy-start.1
  13.4 0.0 copy-start.2
  13.4 8.4 %cell_partial.1 = f32[65,128,128]{2,1,0:T(8,128)S(1)} custom-call(s32[640]{0:T(1024)S(1)} %concatenate.3.index_hbm, bf16[32,128,128]{2,1,0:T(8,128)(2,1)S(1)} %bitcast.10, bf16[512,128,128]{2,1,0:T(8,128)(2,1)} %bitcast.12, f32[65,128,128]{2,1,0:T(8,128)S(1)} %get-tuple-element.8.zero_ref), custom_call_target="tpu_custom_call", output_to_operand_aliasing={{}: (3, {})} | custom-call | flops 2147483648 | bytes 16777216 | tf_op jit(solution)/shard_map/cell_partial/pallas_call | solution.py:178
  21.9 0.0 copy-done.1
  21.9 0.0 copy-done.2
  21.9 22.6 %reduce_mix.1 = bf16[1024,128]{1,0:T(8,128)(2,1)S(1)} custom-call(f32[8320,128]{1,0:T(8,128)S(1)} %bitcast.9, bf16[128,128]{1,0:T(8,128)(2,1)S(1)} %copy-done.1, f32[1,128]{1,0:T(1,128)S(1)} %bitcast.11), custom_call_target="tpu_custom_call" | custom-call | tf_op jit(solution)/shard_map/reduce_mix/pallas_call | solution.py:339
  44.5 0.7 %copy.12 = bf16[1024,128]{1,0:T(8,128)(2,1)} copy(bf16[1024,128]{1,0:T(8,128)(2,1)S(1)} %reduce_mix.1) | data formatting | bytes 524288
  (1 shorter events, 0.0 us)
Async XLA Ops:
  1.4 0.9 %copy-start = (bf16[1024,128]{1,0:T(8,128)(2,1)S(1)}, bf16[1024,128]{1,0:T(8,128)(2,1)}, u32[]{:S(2)}) copy-start(bf16[1024,128]{1,0:T(8,128)(2,1)} %feat_ref.1) | copy-start | bytes 786436
  13.4 8.4 %copy-start.1 = (bf16[128,128]{1,0:T(8,128)(2,1)S(1)}, bf16[128,128]{1,0:T(8,128)(2,1)}, u32[]{:S(2)}) copy-start(bf16[128,128]{1,0:T(8,128)(2,1)} %weight_ref.1) | copy-start | bytes 98308
  13.4 8.4 %copy-start.2 = (f32[128]{0:T(128)S(1)}, f32[128]{0:T(128)}, u32[]{:S(2)}) copy-start(f32[128]{0:T(128)} %param.13) | copy-start | bytes 1540

commit v4 on v3

--- a/solution.py
+++ b/solution.py
@@ -260,7 +260,11 @@
         span = pl.ds(piece * rows, rows)
         return part_ref[mine, :] + pair_buf[dest, span, :].astype(f32)
 
-    for dist in range(line - 1, 0, -1):
+    def pair_start_at(dist):
+        if dist == 0:
+            pair_start(chip)
+            return
+
         @pl.when(chip + dist < line)
         def _():
             pair_start(chip + dist)
@@ -269,7 +273,7 @@
         def _():
             pair_start(chip - dist)
 
-    pair_start(chip)
+    pair_start_at(line - 1)
 
     def forward(dest, piece, upward):
         pair_copy(dest, piece).wait_recv()
@@ -298,6 +302,9 @@
             @pl.when(chip - dist >= 0)
             def _():
                 forward(chip - dist, piece, False)
+
+            if piece == 0:
+                pair_start_at(dist - 1)
 
     for piece in range(PIECES):
         span = pl.ds(piece * rows, rows)

time: 45.4 us -> 45.1 us (level)
  the two profiles are of different devices: /device:TPU:17 before, /device:TPU:0 now
where the time goes in v4:
time: 45.1 us; the launch traced here: 44.9 us
  Pallas kernels  41.8 us (93%)
  local copies, waits for them, and re-layouts  1.67 us (4%)
  other arithmetic  0.71 us (2%)
  between operations  0.71 us (2%)
    pallas_call x1, Pallas kernels, reduce_mix(): pl.pallas_call(functools.partial(reduce_kernel, line, own), out_shape=jax...  20.9 us
    pallas_call x1, Pallas kernels, gather(): pl.pallas_call(kernel, out_shape=(jax.ShapeDtypeStruct((n_row * own, widt...  13.4 us
    pallas_call x1, Pallas kernels, cell_partial(): pl.pallas_call(functools.partial(cell_kernel, slots), out_shape=jax.Shape...  7.55 us
    unnamed x7, local copies, waits for them, and re-layouts  1.67 us

profile of v4, /device:TPU:0, one launch (start us, length us, event | category | flops | bytes accessed | tf_op | source)
XLA Modules:
  0.0 44.9 jit_solution(6557397184627322249)
XLA Ops:
  0.7 0.7 %multiply_add_fusion = s32[512]{0:T(512)S(1)} fusion(s32[512]{0:T(512)} %bitcast.13, s32[512]{0:T(512)} %bitcast.14, s32[]{:T(128)} %bitcast.7), kind=kLoop, calls=%fused_computation | loop fusion | flops 2048 | bytes 6148 | tf_op jit(solution)/shard_map/add | solution.py:175
  1.4 0.0 copy-start
  1.4 0.9 %copy-done = bf16[1024,128]{1,0:T(8,128)(2,1)S(1)} copy-done((bf16[1024,128]{1,0:T(8,128)(2,1)S(1)}, bf16[1024,128]{1,0:T(8,128)(2,1)}, u32[]{:S(2)}) %copy-start) | copy-done | bytes 262168
  2.3 13.4 %gather_band.1 = (bf16[4096,128]{1,0:T(8,128)(2,1)S(1)}, f32[65,128,128]{2,1,0:T(8,128)S(1)}) custom-call(bf16[1024,128]{1,0:T(8,128)(2,1)S(1)} %copy-done), custom_call_target="tpu_custom_call" | custom-call | tf_op jit(solution)/shard_map/gather_band/pallas_call | solution.py:118
  15.7 0.0 copy-start.1
  15.7 0.0 copy-start.2
  15.8 7.6 %cell_partial.1 = f32[65,128,128]{2,1,0:T(8,128)S(1)} custom-call(s32[640]{0:T(1024)S(1)} %concatenate.3.index_hbm, bf16[32,128,128]{2,1,0:T(8,128)(2,1)S(1)} %bitcast.10, bf16[512,128,128]{2,1,0:T(8,128)(2,1)} %bitcast.12, f32[65,128,128]{2,1,0:T(8,128)S(1)} %get-tuple-element.8.zero_ref), custom_call_target="tpu_custom_call", output_to_operand_aliasing={{}: (3, {})} | custom-call | flops 2147483648 | bytes 16777216 | tf_op jit(solution)/shard_map/cell_partial/pallas_call | solution.py:178
  23.3 0.0 copy-done.1
  23.3 0.0 copy-done.2
  23.3 20.9 %reduce_mix.1 = bf16[1024,128]{1,0:T(8,128)(2,1)S(1)} custom-call(f32[8320,128]{1,0:T(8,128)S(1)} %bitcast.9, bf16[128,128]{1,0:T(8,128)(2,1)S(1)} %copy-done.1, f32[1,128]{1,0:T(1,128)S(1)} %bitcast.11), custom_call_target="tpu_custom_call" | custom-call | tf_op jit(solution)/shard_map/reduce_mix/pallas_call | solution.py:346
  44.2 0.7 %copy.12 = bf16[1024,128]{1,0:T(8,128)(2,1)} copy(bf16[1024,128]{1,0:T(8,128)(2,1)S(1)} %reduce_mix.1) | data formatting | bytes 524288
  (1 shorter events, 0.0 us)
Async XLA Ops:
  1.4 0.9 %copy-start = (bf16[1024,128]{1,0:T(8,128)(2,1)S(1)}, bf16[1024,128]{1,0:T(8,128)(2,1)}, u32[]{:S(2)}) copy-start(bf16[1024,128]{1,0:T(8,128)(2,1)} %feat_ref.1) | copy-start | bytes 786436
  15.7 7.6 %copy-start.1 = (bf16[128,128]{1,0:T(8,128)(2,1)S(1)}, bf16[128,128]{1,0:T(8,128)(2,1)}, u32[]{:S(2)}) copy-start(bf16[128,128]{1,0:T(8,128)(2,1)} %weight_ref.1) | copy-start | bytes 98308
  15.7 7.6 %copy-start.2 = (f32[128]{0:T(128)S(1)}, f32[128]{0:T(128)}, u32[]{:S(2)}) copy-start(f32[128]{0:T(128)} %param.13) | copy-start | bytes 1540
